TPU v7x, 1024 devices: a whole 4x4x32 slice. The times are simulated.
1024 devices in a mesh: row: 32 (over z), col: 32 (over y, x, core).
Axes of the slice: x: 4, y: 4, z: 32, core: 2. Of those that a mesh axis runs over, the one named last changes fastest.
Arguments:
- leaf_source: float32 [32, 32, 2, 16, 128], P('row', 'col'), may hold values from -6 to 6
- leaf_pivot: float32 [8192, 8192], P('row', 'col'), may hold values from -0.375 to 0.375
- leaf_update: float32 [16384, 8192], P('row', 'col'), may hold values from -0.09375 to 0.09375
- leaf_targets: int32 [32, 32, 4], P('row', 'col'), may hold values from 0 to 191, as said below
- root_source: float32 [32, 32, 2, 64], P('row', 'col'), may hold values from -6 to 6
- middle_source: float32 [32, 32, 4, 64], P('row', 'col'), may hold values from -6 to 6
- lower_source: float32 [32, 32, 4, 128], P('row', 'col'), may hold values from -6 to 6
- root_pivot: float32 [8192, 8192], P('row', 'col'), may hold values from -0.0625 to 0.0625
- middle_pivot: float32 [8192, 16384], P('row', 'col'), may hold values from -0.0625 to 0.0625
- lower_pivot: float32 [16384, 16384], P('row', 'col'), may hold values from -0.0625 to 0.0625
- middle_update: float32 [4096, 16384], P('row', 'col'), may hold values from -0.09375 to 0.09375
- lower_update: float32 [8192, 16384], P('row', 'col'), may hold values from -0.09375 to 0.09375
- middle_targets: int32 [2, 32], replicated, may hold values from 0 to 63, as said below
- lower_targets: int32 [4, 32], replicated, may hold values from 0 to 127, as said below
Outputs:
- root_solution: float32 [32, 32, 2, 16, 128], P('row', 'col')
- middle_solution: float32 [32, 32, 4, 16, 128], P('row', 'col')
- lower_solution: float32 [32, 32, 4, 16, 128], P('row', 'col')
- leaf_solution: float32 [32, 32, 2, 16, 128], P('row', 'col')
Inputs may be any that keep to these rules, and one draw needn't show every extreme that they name: `middle_targets`: the 32 entries of a row are different root blocks. `lower_targets`: the 32 entries of a row are different chain blocks of the root and the parent front. `leaf_targets`: the 4 entries of a device are different chain blocks.
All inputs are finite; a program needn't handle non-finite values.
Results may differ from a plain program's by a relative error of at most 0.00013.
Values sent between devices are 32-bit elements; how exact they have to be, the bound alone decides.
A program may use at most 32 MiB of HBM per device.

v0:
```python
import jax
import jax.numpy as jnp
from jax import lax
from jax.sharding import PartitionSpec as P

precise = lax.Precision.HIGHEST


def apply_tile(matrix, vector):
    block_width = vector.shape[2]
    out_tiles = matrix.shape[0] // block_width
    shaped = matrix.reshape(out_tiles, block_width, vector.shape[0], block_width)
    return jnp.einsum("pAqb,qkb->pkA", shaped, vector, precision=precise)


def apply_transposed(matrix, vector):
    block_width = vector.shape[2]
    in_tiles = matrix.shape[1] // block_width
    shaped = matrix.reshape(vector.shape[0], block_width, in_tiles, block_width)
    return jnp.einsum("pAqb,pkA->qkb", shaped, vector, precision=precise)


def one_hot(targets, table_width):
    return (targets[:, None] == jnp.arange(table_width, dtype=jnp.int32)[None, :]).astype(
        jnp.float32
    )


def scatter_blocks(targets, values, table_width):
    return jnp.einsum("ns,nkb->skb", one_hot(targets, table_width), values, precision=precise)


def fetch_blocks(targets, chain_blocks):
    return jnp.einsum(
        "ns,skb->nkb", one_hot(targets, chain_blocks.shape[0]), chain_blocks, precision=precise
    )


def pick_slot(summed, slot_index):
    return lax.dynamic_index_in_dim(summed, slot_index, 0, keepdims=False)


def slotted(operand, slot_count, slot_index):
    selector = (jnp.arange(slot_count, dtype=jnp.int32) == slot_index).astype(operand.dtype)
    return selector.reshape((slot_count,) + (1,) * operand.ndim) * operand[None]


def row_total(operand, group_rows):
    slot_index = lax.axis_index("row") // group_rows
    summed = lax.psum(slotted(operand, lax.axis_size("row") // group_rows, slot_index), "row")
    return pick_slot(summed, slot_index)


def column_total(operand, group_cols):
    slot_index = lax.axis_index("col") // group_cols
    summed = lax.psum(slotted(operand, lax.axis_size("col") // group_cols, slot_index), "col")
    return pick_slot(summed, slot_index)


def spread_columns(solution, group_cols):
    col_count = lax.axis_size("col")
    gathered = lax.all_gather(solution, "col", axis=0, tiled=True)
    col_tiles = solution.shape[0]
    shaped = gathered.reshape(
        col_count // group_cols, group_cols, col_tiles, solution.shape[1], solution.shape[2]
    )
    own_group = pick_slot(shaped, lax.axis_index("col") // group_cols)
    return jnp.transpose(own_group, (1, 0, 2, 3)).reshape(
        col_tiles * group_cols, solution.shape[1], solution.shape[2]
    )


def reduce_level(partial_value, source, group_rows, group_cols):
    col_count = lax.axis_size("col")
    col_index = lax.axis_index("col")
    source_count = partial_value.shape[1]
    block_width = partial_value.shape[2]
    col_tiles = partial_value.shape[0] // group_cols
    arranged = jnp.transpose(
        partial_value.reshape(col_tiles, group_cols, source_count, block_width), (1, 0, 2, 3)
    )
    operand = slotted(arranged, col_count // group_cols, col_index // group_cols)
    column_sum = lax.psum_scatter(
        operand.reshape(col_count * col_tiles, source_count, block_width),
        "col",
        scatter_dimension=0,
        tiled=True,
    )
    piece_length = source.shape[-1]
    offset = lax.axis_index("row") % group_rows * piece_length
    flat_source = lax.dynamic_update_slice(
        jnp.zeros((col_tiles, source_count * block_width), jnp.float32),
        source[0, 0],
        (jnp.int32(0), offset),
    )
    placed = flat_source.reshape(col_tiles, source_count, block_width)
    return row_total(placed - column_sum, group_rows)


def own_targets(targets, front_index, update_tiles, group_rows):
    row_here = (
        jnp.arange(update_tiles, dtype=jnp.int32) * group_rows + lax.axis_index("row") % group_rows
    )
    target_row = lax.dynamic_index_in_dim(targets, front_index, 0, keepdims=False)
    return jnp.take(target_row, row_here)


def local(
    leaf_source,
    leaf_pivot,
    leaf_update,
    leaf_targets,
    root_source,
    middle_source,
    lower_source,
    root_pivot,
    middle_pivot,
    lower_pivot,
    middle_update,
    lower_update,
    middle_targets,
    lower_targets,
):
    row_count = lax.axis_size("row")
    col_count = lax.axis_size("col")
    root_rows, root_cols = (row_count, col_count)
    middle_rows, middle_cols = (row_count, col_count // 2)
    lower_rows, lower_cols = (row_count // 2, col_count // 2)
    sep_count = root_source.shape[2] * col_count
    block_width = leaf_source.shape[4]
    middle_front = lax.axis_index("col") // middle_cols
    lower_front = 2 * middle_front + lax.axis_index("row") // lower_rows
    leaf_vector = leaf_source[0, 0]
    leaf_forward = apply_tile(leaf_pivot, leaf_vector)
    chain_sums = scatter_blocks(
        leaf_targets[0, 0], apply_tile(leaf_update, leaf_vector), 3 * sep_count
    )
    lower_input = reduce_level(chain_sums[2 * sep_count :], lower_source, lower_rows, lower_cols)
    lower_partial = apply_tile(lower_pivot, lower_input)
    lower_ids = own_targets(
        lower_targets, lower_front, lower_update.shape[0] // block_width, lower_rows
    )
    chain_sums = chain_sums + scatter_blocks(
        lower_ids, apply_tile(lower_update, lower_input), 3 * sep_count
    )
    middle_input = reduce_level(
        chain_sums[sep_count : 2 * sep_count], middle_source, middle_rows, middle_cols
    )
    middle_partial = apply_tile(middle_pivot, middle_input)
    middle_ids = own_targets(
        middle_targets, middle_front, middle_update.shape[0] // block_width, middle_rows
    )
    chain_sums = chain_sums + scatter_blocks(
        middle_ids, apply_tile(middle_update, middle_input), 3 * sep_count
    )
    root_input = reduce_level(chain_sums[:sep_count], root_source, root_rows, root_cols)
    root_partial = apply_tile(root_pivot, root_input)
    root_forward = column_total(root_partial, root_cols)
    middle_forward = column_total(middle_partial, middle_cols)
    lower_forward = column_total(lower_partial, lower_cols)
    root_answer = row_total(apply_transposed(root_pivot, root_forward), root_rows)
    root_chain = spread_columns(root_answer, root_cols)
    middle_terms = apply_transposed(middle_pivot, middle_forward) - apply_transposed(
        middle_update, fetch_blocks(middle_ids, root_chain)
    )
    middle_answer = row_total(middle_terms, middle_rows)
    upper_chain = jnp.concatenate([root_chain, spread_columns(middle_answer, middle_cols)], axis=0)
    lower_terms = apply_transposed(lower_pivot, lower_forward) - apply_transposed(
        lower_update, fetch_blocks(lower_ids, upper_chain)
    )
    lower_answer = row_total(lower_terms, lower_rows)
    full_chain = jnp.concatenate([upper_chain, spread_columns(lower_answer, lower_cols)], axis=0)
    leaf_answer = apply_transposed(leaf_pivot, leaf_forward) - apply_transposed(
        leaf_update, fetch_blocks(leaf_targets[0, 0], full_chain)
    )
    return (
        root_answer[None, None],
        middle_answer[None, None],
        lower_answer[None, None],
        leaf_answer[None, None],
    )


def solution(mesh):
    placed = (
        P("row", "col", None, None, None),
        P("row", "col"),
        P("row", "col"),
        P("row", "col", None),
        P("row", "col", None, None),
        P("row", "col", None, None),
        P("row", "col", None, None),
        P("row", "col"),
        P("row", "col"),
        P("row", "col"),
        P("row", "col"),
        P("row", "col"),
        P(),
        P(),
    )
    return jax.shard_map(
        local,
        mesh=mesh,
        in_specs=placed,
        out_specs=(
            P("row", "col", None, None, None),
            P("row", "col", None, None, None),
            P("row", "col", None, None, None),
            P("row", "col", None, None, None),
        ),
        check_vma=False,
    )
```

profile of v0, /device:TPU:1, one launch (start us, length us, event | category | flops | bytes accessed | tf_op | source)
XLA Modules:
  0.0 1812.9 jit_solution(14875619312518264831)
XLA Ops:
  7.4 1.3 reshape.218
  8.8 1.2 convolution_bitcast_fusion.4
  10.0 1.0 fusion.44
  11.3 1.2 bitcast_multiply_fusion.1
  14.0 137.8 %reduce-scatter.4.cloned.1.call-done = f32[4,16,128]{2,1,0:T(8,128)} async-done(((f32[128,16,128]{2,1,0:T(8,128)}), f32[4,16,128]{2,1,0:T(8,128)}) %reduce-scatter.4.cloned.1.call-update) | async-done | bytes 32784 | tf_op jit(solution)/shard_map/reduce_scatter | solution.py:83
  153.5 229.2 %all-reduce.5.cloned.1.call-done = f32[2,4,16,128]{3,2,0,1:T(8,128)} async-done(((f32[2,4,16,128]{3,2,0,1:T(8,128)}), f32[2,4,16,128]{3,2,0,1:T(8,128)}) %all-reduce.5.cloned.1.call-update) | async-done | bytes 65552 | tf_op jit(solution)/shard_map/psum | solution.py:50
  382.7 1.3 convolution_bitcast_fusion.11
  384.0 1.0 convolution_add_fusion
  385.0 1.1 copy-done.1
  386.5 1.2 bitcast_multiply_fusion
  389.3 138.6 %reduce-scatter.6.cloned.1.call-done = f32[4,16,128]{2,1,0:T(8,128)} async-done(((f32[128,16,128]{2,1,0:T(8,128)}), f32[4,16,128]{2,1,0:T(8,128)}) %reduce-scatter.6.cloned.1.call-update) | async-done | bytes 32784 | tf_op jit(solution)/shard_map/reduce_scatter | solution.py:83
  528.7 83.6 %psum.64 = f32[4,16,128]{2,1,0:T(8,128)S(1)} all-reduce(f32[4,16,128]{2,1,0:T(8,128)S(1)} %fusion.37), channel_id=1, replica_groups=mesh['row'=32,'col'=32] {'row'}, use_global_device_ids=true, to_apply=%region_3.4 | all-reduce | flops 8192 | bytes 65536 | tf_op jit(solution)/shard_map/psum | solution.py:50
  612.6 1.3 fusion.22
  613.9 1.1 copy.83
  616.2 150.5 %reduce-scatter.8.cloned.1.call-done = f32[2,16,128]{2,1,0:T(8,128)} async-done(((f32[64,16,128]{2,1,0:T(8,128)}), f32[2,16,128]{2,1,0:T(8,128)}) %reduce-scatter.8.cloned.1.call-update) | async-done | bytes 16400 | tf_op jit(solution)/shard_map/reduce_scatter | solution.py:83
  767.4 83.4 %psum.65 = f32[2,16,128]{2,1,0:T(8,128)S(1)} all-reduce(f32[2,16,128]{2,1,0:T(8,128)S(1)} %fusion.49), channel_id=1, replica_groups=mesh['row'=32,'col'=32] {'row'}, use_global_device_ids=true, to_apply=%region_5.6 | all-reduce | flops 4096 | bytes 32768 | tf_op jit(solution)/shard_map/psum | solution.py:50
  851.1 147.2 %all-reduce = (f32[2,16,128]{2,1,0:T(8,128)S(1)}, f32[2,2,16,128]{3,2,1,0:T(8,128)S(1)}) all-reduce(f32[2,16,128]{2,1,0:T(8,128)S(1)} %fusion.15, f32[2,2,16,128]{3,2,1,0:T(8,128)S(1)} %broadcast_multiply_fusion.3), channel_id=1, replica_groups=mesh['row'=32,'col'=32] {'col'}, use_global_device_ids=true, to_apply=%region_6.7 | all-reduce | flops 12288 | bytes 98304 | tf_op jit(solution)/shard_map/psum | solution.py:56
  998.6 78.0 %psum.67 = f32[1,2,16,128]{3,2,1,0:T(8,128)S(1)} all-reduce(f32[1,2,16,128]{3,2,1,0:T(8,128)S(1)} %fusion.13), channel_id=1, replica_groups=mesh['row'=32,'col'=32] {'row'}, use_global_device_ids=true, to_apply=%region_7.8 | all-reduce | flops 4096 | bytes 32768 | tf_op jit(solution)/shard_map/psum | solution.py:50
  1076.6 54.5 %all-gather = f32[1,64,16,128]{3,2,0,1:T(8,128)S(1)} all-gather(f32[1,2,16,128]{3,2,0,1:T(8,128)S(1)} %bitcast.228), channel_id=2, replica_groups=mesh['row'=32,'col'=32] {'col'}, dimensions={1}, use_global_device_ids=true | all-gather | bytes 540672 | tf_op jit(solution)/shard_map/all_gather | solution.py:62
  1132.2 78.5 %psum.69 = f32[1,4,16,128]{3,2,1,0:T(8,128)} all-reduce(f32[1,4,16,128]{3,2,1,0:T(8,128)S(1)} %fusion.9), channel_id=1, replica_groups=mesh['row'=32,'col'=32] {'row'}, use_global_device_ids=true, to_apply=%region_9.10 | all-reduce | flops 8192 | bytes 65536 | tf_op jit(solution)/shard_map/psum | solution.py:50
  1210.8 1.6 reshape.229
  1212.4 1.0 convolution_bitcast_fusion.1
  1214.5 95.2 %all-gather.6.cloned.1.call-done = f32[1,128,16,128]{3,2,0,1:T(8,128)} async-done(((f32[1,4,16,128]{3,2,0,1:T(8,128)}), f32[1,128,16,128]{3,2,0,1:T(8,128)}) %all-gather.6.cloned.1.call-update) | async-done | bytes 1048592 | tf_op jit(solution)/shard_map/all_gather | solution.py:62
  1309.7 1.1 constant_dynamic-slice_fusion.1
  1311.8 169.8 %all-reduce.7.cloned.1.call-done = f32[2,4,16,128]{3,2,1,0:T(8,128)} async-done(((f32[2,4,16,128]{3,2,1,0:T(8,128)}), f32[2,4,16,128]{3,2,1,0:T(8,128)}) %all-reduce.7.cloned.1.call-update) | async-done | bytes 65552 | tf_op jit(solution)/shard_map/psum | solution.py:56
  1481.7 1.4 fusion.7
  1483.8 225.2 %all-reduce.9.cloned.1.call-done = f32[2,4,16,128]{3,2,0,1:T(8,128)} async-done(((f32[2,4,16,128]{3,2,0,1:T(8,128)}), f32[2,4,16,128]{3,2,0,1:T(8,128)}) %all-reduce.9.cloned.1.call-update) | async-done | bytes 65552 | tf_op jit(solution)/shard_map/psum | solution.py:50
  1708.9 1.4 constant_dynamic-slice_fusion
  1710.3 1.1 reshape.232
  1711.7 1.4 fusion.89
  1713.1 89.8 %all-gather.8.cloned.1.call-done = f32[1,128,16,128]{3,2,0,1:T(8,128)} async-done(((f32[1,4,16,128]{3,2,0,1:T(8,128)}), f32[1,128,16,128]{3,2,0,1:T(8,128)}) %all-gather.8.cloned.1.call-update) | async-done | bytes 1048592 | tf_op jit(solution)/shard_map/all_gather | solution.py:62
  1802.9 1.1 constant_dynamic-slice_fusion.2
  (92 shorter events, 14.6 us)
Async XLA Ops:
  7.2 605.2 %copy-start = (f32[128,512]{1,0:T(8,128)S(1)}, f32[128,512]{1,0:T(8,128)}, u32[]{:S(2)}) copy-start(f32[128,512]{1,0:T(8,128)} %param.24) | copy-start | bytes 786436
  7.2 2.8 copy-start.11
  7.2 144.6 %reduce-scatter.4.cloned.1.call-start = ((), (), s32[]{:S(2)}) async-start(), calls=%async_computation.3 | async-start | bytes 1081344 | tf_op jit(solution)/shard_map/reduce_scatter | solution.py:83
  11.3 2.7 copy-start.8
  11.3 142.0 %copy-start.2 = (f32[256,512]{1,0:T(8,128)S(1)}, f32[256,512]{1,0:T(8,128)}, u32[]{:S(2)}) copy-start(f32[256,512]{1,0:T(8,128)} %param.25) | copy-start | bytes 1572868
  12.6 370.2 %all-reduce.5.cloned.1.call-start = ((), (), s32[]{:S(2)}) async-start(), calls=%async_computation.4 | async-start | bytes 131072 | tf_op jit(solution)/shard_map/psum | solution.py:50
  153.3 374.7 %reduce-scatter.6.cloned.1.call-start = ((), (), s32[]{:S(2)}) async-start(), calls=%async_computation.5 | async-start | bytes 1081344 | tf_op jit(solution)/shard_map/reduce_scatter | solution.py:83
  385.0 1.2 copy-start.1
  386.5 1.3 copy-start.12
  386.5 2.6 copy-start.9
  387.7 379.0 %reduce-scatter.8.cloned.1.call-start = ((), (), s32[]{:S(2)}) async-start(), calls=%async_computation.6 | async-start | bytes 540672 | tf_op jit(solution)/shard_map/reduce_scatter | solution.py:83
  389.1 226.0 %copy-start.4 = (f32[256,256]{1,0:T(8,128)S(1)}, f32[256,256]{1,0:T(8,128)}, u32[]{:S(2)}) copy-start(f32[256,256]{1,0:T(8,128)} %param.21) | copy-start | bytes 786436
  612.6 2.6 copy-start.3
  613.9 1.6 copy-start.10
  615.0 694.6 %all-gather.6.cloned.1.call-start = ((), (), s32[]{:S(2)}) async-start(), calls=%async_computation.9 | async-start | bytes 1081344 | tf_op jit(solution)/shard_map/all_gather | solution.py:62
  1076.6 134.1 %copy-start.6 = (f32[1,2,16,128]{3,2,1,0:T(8,128)}, f32[1,2,16,128]{3,2,1,0:T(8,128)S(1)}, u32[]{:S(2)}) copy-start(f32[1,2,16,128]{3,2,1,0:T(8,128)S(1)} %psum.67) | copy-start | bytes 49156
  1131.6 80.8 %copy-start.7 = (f32[2,4,16,128]{3,2,0,1:T(8,128)S(1)}, f32[2,4,16,128]{3,2,0,1:T(8,128)}, u32[]{:S(2)}) copy-start(f32[2,4,16,128]{3,2,0,1:T(8,128)} %all-reduce.5.cloned.1.call-done) | copy-start | bytes 196612
  1210.7 270.9 %all-reduce.7.cloned.1.call-start = ((), (), s32[]{:S(2)}) async-start(), calls=%async_computation.7 | async-start | bytes 131072 | tf_op jit(solution)/shard_map/psum | solution.py:56
  1214.1 494.9 %all-reduce.9.cloned.1.call-start = ((), (), s32[]{:S(2)}) async-start(), calls=%async_computation.8 | async-start | bytes 131072 | tf_op jit(solution)/shard_map/psum | solution.py:50
  1311.0 400.4 %copy-start.5 = (f32[1,1,2,16,128]{4,3,2,1,0:T(8,128)S(1)}, f32[1,1,2,16,128]{4,3,2,1,0:T(8,128)}, u32[]{:S(2)}) copy-start(f32[1,1,2,16,128]{4,3,2,1,0:T(8,128)} %param.14) | copy-start | bytes 49156
  1483.7 319.2 %all-gather.8.cloned.1.call-start = ((), (), s32[]{:S(2)}) async-start(), calls=%async_computation.10 | async-start | bytes 1081344 | tf_op jit(solution)/shard_map/all_gather | solution.py:62
Sparse Core Ops, SparseCore 0:
  13.6 138.1 reduce-scatter.3
  154.2 228.4 all-reduce.4
  388.3 139.5 reduce-scatter.5
  615.2 151.5 reduce-scatter.7
  1210.9 98.7 all-gather.5
  1313.1 168.4 all-reduce.6
  1484.0 224.9 all-reduce.8
  1714.0 88.8 all-gather.7
where the time goes:
time: 1810 us
  waiting for transfers between devices  1240 us (69%)
  blocking collectives  525 us (29%)
    psum x2, waiting for transfers between devices, row_total(): lax.psum(slotted(operand, lax.axis_size('row') // group_rows, slot_index)...  454 us
    reduce_scatter x3, waiting for transfers between devices, reduce_level(): lax.psum_scatter(operand.reshape(col_count * col_tiles, source_count, blo...  427 us
    psum x4, blocking collectives, row_total(): lax.psum(slotted(operand, lax.axis_size('row') // group_rows, slot_index)...  324 us
    all_gather x2, waiting for transfers between devices, spread_columns(): gathered = lax.all_gather(solution, 'col', axis=0, tiled=True)  185 us
    psum x1, waiting for transfers between devices, column_total(): lax.psum(slotted(operand, lax.axis_size('col') // group_cols, slot_index)...  170 us
    psum x1, blocking collectives, column_total(): lax.psum(slotted(operand, lax.axis_size('col') // group_cols, slot_index)...  147 us
    all_gather x1, blocking collectives, spread_columns(): gathered = lax.all_gather(solution, 'col', axis=0, tiled=True)  54.5 us
  transfers between devices with their start and end apart: 8, of which 8 were waited for; matrix products, arithmetic and copies ran while one was open for 1% of the time, Pallas kernels for 0%

commit v1 on v0

v1 whole, which is shorter than its diff:
```python
import jax
import jax.numpy as jnp
from jax import lax
from jax.experimental import pallas as pl
from jax.experimental.pallas import tpu as pltpu
from jax.sharding import PartitionSpec as P

MESH = pl.DeviceIdType.MESH
F32 = jnp.float32
BF16 = jnp.bfloat16

PHASES = {
    "targets": ("row16", 1),
    "leaf_send": ("row16", 4),
    "middle_source": ("row32", 2),
    "root_source": ("row32", 1),
    "low_sum": ("col16", 4),
    "mid_sum": ("col16", 4),
    "root_sum": ("col32", 2),
    "low_input": ("row16", 4),
    "mid_base": ("row32", 4),
    "root_base": ("row32", 2),
    "low_update": ("col16", 2),
    "low_product": ("col16", 4),
    "low_forward": ("col16", 4),
    "low_spread": ("row32", 2),
    "mid_input": ("col16", 4),
    "mid_update": ("col16", 1),
    "mid_product": ("col16", 2),
    "mid_forward": ("col16", 2),
    "mid_spread": ("row32", 1),
    "root_input": ("col32", 2),
    "root_product": ("col32", 1),
    "root_forward": ("col32", 1),
    "root_terms": ("col32", 2),
    "mid_fetch": ("row32", 1),
    "mid_fetched": ("col16", 1),
    "root_rows": ("row32", 1),
    "root_out": ("row32", 1),
    "root_chain": ("col32", 2),
    "mid_terms": ("col16", 4),
    "low_fetch": ("row32", 2),
    "low_fetched": ("col16", 2),
    "mid_rows": ("row32", 2),
    "mid_out": ("row32", 2),
    "mid_chain": ("col16", 4),
    "low_rows": ("row16", 4),
    "low_chain": ("col16", 4),
    "low_out": ("row16", 4),
    "leaf_fetch": ("row16", 4),
}
NAMES = list(PHASES)
COUNT = {"row16": 16, "row32": 32, "col16": 16, "col32": 32}

SOURCES_OF = {
    "targets": 1,
    "leaf_send": 64,
    "middle_source": 2,
    "root_source": 1,
    "low_sum": 64,
    "mid_sum": 64,
    "root_sum": 64,
    "low_input": 4,
    "mid_base": 4,
    "root_base": 2,
    "low_update": 32,
    "low_product": 64,
    "low_forward": 4,
    "low_spread": 2,
    "mid_input": 64,
    "mid_update": 16,
    "mid_product": 32,
    "mid_forward": 2,
    "mid_spread": 1,
    "root_input": 64,
    "root_product": 32,
    "root_forward": 1,
    "root_terms": 32,
    "mid_fetch": 32,
    "mid_fetched": 1,
    "root_rows": 32,
    "root_out": 1,
    "root_chain": 2,
    "mid_terms": 64,
    "low_fetch": 64,
    "low_fetched": 2,
    "mid_rows": 64,
    "mid_out": 2,
    "mid_chain": 4,
    "low_rows": 64,
    "low_chain": 4,
    "low_out": 4,
    "leaf_fetch": 64,
}

MATRICES = {
    "leaf_update": (512, 256),
    "leaf_pivot": (256, 256),
    "lower_update": (256, 512),
    "lower_pivot": (512, 512),
    "middle_update": (128, 512),
    "middle_pivot": (256, 512),
    "root_pivot": (256, 256),
}


def halves(value):
    high = value.astype(BF16)
    return high, (value - high.astype(F32)).astype(BF16)


def product(vector, high, low, contract):
    vector_high, vector_low = halves(vector)
    dims = (((1,), (contract,)), ((), ()))
    both = lax.dot_general(
        jnp.concatenate([vector_high, vector_low], axis=0), high, dims, preferred_element_type=F32
    )
    rest = lax.dot_general(vector_high, low, dims, preferred_element_type=F32)
    return both[:16] + (both[16:] + rest)


def pick(selector, blocks):
    high, low = halves(blocks)
    return jnp.dot(selector, high, preferred_element_type=F32) + jnp.dot(
        selector, low, preferred_element_type=F32
    )


def as_float(condition):
    return jnp.where(condition, 1.0, 0.0).astype(BF16)


def flipped(selector):
    count = selector.shape[1]
    rows = lax.broadcasted_iota(jnp.int32, (count, count), 0)
    cols = lax.broadcasted_iota(jnp.int32, (count, count), 1)
    return lax.dot_general(
        as_float(rows == cols), selector, (((1,), (1,)), ((), ())), preferred_element_type=F32
    ).astype(BF16)


def root_numbers(width):
    slot = lax.broadcasted_iota(jnp.int32, (64, width), 0)
    return (slot & 1) * 32 + (slot >> 1)


def group_numbers(width):
    slot = lax.broadcasted_iota(jnp.int32, (64, width), 0)
    return (slot & 3) * 16 + (slot >> 2)


def kernel(
    leaf_source,
    leaf_targets,
    root_source,
    middle_source,
    lower_source,
    middle_targets,
    lower_targets,
    *rest,
):
    in_hbm = dict(zip(MATRICES, rest[:7]))
    root_solution, middle_solution, lower_solution, leaf_solution = rest[7:11]
    rest = rest[11:]
    loaded = dict(zip(MATRICES, rest[:7]))
    high = dict(zip(MATRICES, rest[7:14]))
    low = dict(zip(MATRICES, rest[14:21]))
    rest = rest[21:]
    out_of = dict(zip(NAMES, rest[: len(NAMES)]))
    into = dict(zip(NAMES, rest[len(NAMES) : 2 * len(NAMES)]))
    send_sem, recv_sem, load_sem = rest[2 * len(NAMES) :]

    r = lax.axis_index("row")
    c = lax.axis_index("col")
    half = c // 16
    i16 = r % 16
    j16 = c % 16
    y, x, core = c // 8, (c // 2) % 4, c % 2
    my_place = {"row16": i16, "row32": r, "col16": j16, "col32": c}

    def peer(kind, step):
        if kind == "row32":
            odd = step % 2
            place = (r + 16 + (2 * odd - 1) * ((step + 1) // 2)) % 32
            return place, (place, c)
        if kind == "row16":
            back = i16 // 8
            own = i16 * back + (15 - i16) * (1 - back)
            at = step + jnp.where(step >= own, 1, 0)
            place = at * back + (15 - at) * (1 - back)
            return place, (r - i16 + place, c)
        if kind == "col16":
            at = step + jnp.where(step >= 13, 1, 0)
            there_y = (y % 2 + 1 + at // 8) % 2
            there_x = (x + 2 + at // 2) % 4
            there_core = (core + 1 + at) % 2
            place = there_y * 8 + there_x * 2 + there_core
            return place, (r, half * 16 + place)
        at = step + jnp.where(step >= 21, 1, 0)
        there_y = (y + 2 + at // 8) % 4
        there_x = (x + 2 + at // 2) % 4
        there_core = (core + 1 + at) % 2
        place = there_y * 8 + there_x * 2 + there_core
        return place, (r, place)

    def send(name, each=None):
        kind, rows = PHASES[name]
        index = NAMES.index(name)
        source, target = out_of[name], into[name]

        def piece(place):
            return source.at[pl.ds(0 if each is None else each(place) * rows, rows)]

        here = target.at[pl.ds(my_place[kind] * rows, rows)]

        def one(step, carry):
            place, device = peer(kind, step)
            pltpu.make_async_remote_copy(
                src_ref=piece(place),
                dst_ref=here,
                send_sem=send_sem.at[index],
                recv_sem=recv_sem.at[index],
                device_id=device,
                device_id_type=MESH,
            ).start()
            return carry

        lax.fori_loop(0, COUNT[kind] - 1, one, 0)
        pltpu.make_async_copy(piece(my_place[kind]), here, recv_sem.at[index]).start()

    def arrived(name):
        buffer = into[name]
        pltpu.make_async_copy(buffer, buffer, recv_sem.at[NAMES.index(name)]).wait()
        return buffer

    def total(name):
        kind, rows = PHASES[name]
        buffer = arrived(name)
        parts = [buffer[pl.ds(8 * at, 8), :] for at in range(COUNT[kind] * rows // 8)]
        while len(parts) > 1:
            parts = [a + b for a, b in zip(parts[::2], parts[1::2])]
        value = parts[0]
        size = 8
        while size > rows:
            size //= 2
            value = value[:size] + value[size:]
        return value

    def wide(buffer, rows, start=0):
        return jnp.concatenate(
            [buffer[pl.ds(start + at, 16, stride=rows), :] for at in range(rows)], axis=1
        )

    def put(name, value):
        rows = value.shape[1] // 128
        buffer = out_of[name]
        if rows == 1:
            buffer[...] = value
        else:
            for at in range(rows):
                buffer[pl.ds(at, 16, stride=rows), :] = value[:, at * 128 : (at + 1) * 128]

    def stacked(name, value):
        for at in range(value.shape[1] // 128):
            out_of[name][pl.ds(at * 16, 16), :] = value[:, at * 128 : (at + 1) * 128]

    def load(name):
        index = list(MATRICES).index(name)
        return pltpu.make_async_copy(in_hbm[name], loaded[name], load_sem.at[index])

    def split(name):
        load(name).wait()
        high[name][...], low[name][...] = halves(loaded[name][...])

    def apply(name, vector):
        return product(vector, high[name][...], low[name][...], 1)

    def apply_transposed(name, vector):
        return product(vector, high[name][...], low[name][...], 0)

    same = lambda place: place

    for name in MATRICES:
        load(name).start()

    barrier = pltpu.get_barrier_semaphore()
    for kind in ("row32", "col32"):

        def greet(step, carry, kind=kind):
            pl.semaphore_signal(
                barrier, inc=1, device_id=peer(kind, step)[1], device_id_type=MESH
            )
            return carry

        lax.fori_loop(0, 31, greet, 0)

    lane = lax.broadcasted_iota(jnp.int32, (1, 128), 1)
    own_row = jnp.zeros((1, 128), F32)
    for m in range(4):
        own_row = jnp.where(lane == 4 * i16 + m, leaf_targets[0, 0, m].astype(F32), own_row)
    out_of["targets"][...] = own_row
    mid_src = middle_source[0, 0]
    out_of["middle_source"][...] = jnp.concatenate(
        [
            jnp.concatenate([mid_src[0:1], mid_src[1:2]], axis=1),
            jnp.concatenate([mid_src[2:3], mid_src[3:4]], axis=1),
        ],
        axis=0,
    )
    root_src = root_source[0, 0]
    out_of["root_source"][...] = jnp.concatenate([root_src[0:1], root_src[1:2]], axis=1)

    leaf_vector = jnp.concatenate([leaf_source[0, 0, 0], leaf_source[0, 0, 1]], axis=1)
    split("leaf_update")
    put("leaf_send", apply("leaf_update", leaf_vector))

    pl.semaphore_wait(barrier, 62)
    send("targets")
    send("leaf_send", same)
    send("middle_source")
    send("root_source")

    for name in list(MATRICES)[1:]:
        split(name)
    leaf_terms = apply_transposed("leaf_pivot", apply("leaf_pivot", leaf_vector))

    mid_target = middle_targets[pl.ds(half, 1), :]
    mid_place = as_float(root_numbers(32) == mid_target)
    mid_place_flip = flipped(mid_place)
    update_row = lax.broadcasted_iota(jnp.int32, (32, 64), 0)
    slot = lax.broadcasted_iota(jnp.int32, (32, 64), 1)
    order = (update_row & 15) * 2 + (update_row >> 4)
    low_target = jnp.zeros((8, 64), F32)
    for part in range(2):
        values = lower_targets[pl.ds(2 * half + part, 1), :].astype(F32)
        low_target = low_target + jnp.dot(
            jnp.broadcast_to(values, (8, 32)).astype(BF16),
            as_float(slot == order + 32 * part),
            preferred_element_type=F32,
        )
    low_target = low_target[0:1]
    low_place_root = as_float(root_numbers(64).astype(F32) == low_target)
    low_place_mid = as_float((group_numbers(64) + 64).astype(F32) == low_target)
    low_place_root_flip = flipped(low_place_root)
    low_place_mid_flip = flipped(low_place_mid)

    leaf_target = jnp.sum(arrived("targets")[...], axis=0, keepdims=True)[:, :64]
    leaf_place_low = as_float((group_numbers(64) + 128).astype(F32) == leaf_target)
    sent = arrived("leaf_send")[...]
    out_of["low_sum"][...] = pick(leaf_place_low, sent)
    send("low_sum", same)
    leaf_place_mid = as_float((group_numbers(64) + 64).astype(F32) == leaf_target)
    leaf_place_root = as_float(root_numbers(64).astype(F32) == leaf_target)
    out_of["mid_sum"][...] = pick(leaf_place_mid, sent)
    send("mid_sum", same)

    out_of["low_input"][...] = lower_source[0, 0] - total("low_sum")
    send("low_input")
    out_of["root_sum"][...] = pick(leaf_place_root, sent)
    send("root_sum", same)
    out_of["mid_base"][...] = total("mid_sum")
    send("mid_base")
    leaf_place_low_flip = flipped(leaf_place_low)
    leaf_place_mid_flip = flipped(leaf_place_mid)
    leaf_place_root_flip = flipped(leaf_place_root)
    out_of["root_base"][...] = total("root_sum")

    low_vector = wide(arrived("low_input"), 4)
    put("low_update", apply("lower_update", low_vector))
    send("low_update", same)
    put("low_product", apply("lower_pivot", low_vector))
    out_of["low_spread"][...] = total("low_update")
    send("low_spread")
    send("low_product", same)
    send("root_base")
    out_of["low_forward"][...] = total("low_product")
    send("low_forward")
    upper_lane = lax.broadcasted_iota(jnp.int32, (16, 128), 1) >= 64
    source_rows = arrived("middle_source")
    mid_base = []
    for pair in range(2):
        even = source_rows[pl.ds(pair, 16, stride=4), :]
        odd = source_rows[pl.ds(2 + pair, 16, stride=4), :]
        mid_base.append(jnp.where(upper_lane, pltpu.roll(odd, 64, 1), even))
        mid_base.append(jnp.where(upper_lane, odd, pltpu.roll(even, 64, 1)))
    sums = arrived("mid_base")
    mid_base = jnp.concatenate(mid_base, axis=1) - (wide(sums, 4) + wide(sums, 4, 64))
    low_terms = apply_transposed("lower_pivot", wide(arrived("low_forward"), 4))

    updates = arrived("low_spread")[...]
    out_of["mid_input"][...] = pick(low_place_mid, updates)
    send("mid_input", same)
    root_updates = pick(low_place_root, updates)
    mid_vector = mid_base - wide(arrived("mid_input"), 4)
    put("mid_update", apply("middle_update", mid_vector))
    send("mid_update", same)
    put("mid_product", apply("middle_pivot", mid_vector))
    out_of["mid_spread"][...] = total("mid_update")
    send("mid_spread")
    send("mid_product", same)
    out_of["mid_forward"][...] = total("mid_product")
    send("mid_forward")
    source_rows = arrived("root_source")
    even = source_rows[pl.ds(0, 16, stride=2), :]
    odd = source_rows[pl.ds(1, 16, stride=2), :]
    root_base = jnp.concatenate(
        [
            jnp.where(upper_lane, pltpu.roll(odd, 64, 1), even),
            jnp.where(upper_lane, odd, pltpu.roll(even, 64, 1)),
        ],
        axis=1,
    )
    sums = arrived("root_base")
    root_base = root_base - (wide(sums, 2) + wide(sums, 2, 32))
    mid_terms = apply_transposed("middle_pivot", wide(arrived("mid_forward"), 2))

    out_of["root_input"][...] = root_updates + pick(mid_place, arrived("mid_spread")[...])
    send("root_input", same)
    sums = arrived("root_input")
    root_vector = root_base - (wide(sums, 2) + wide(sums, 2, 32))
    stacked("root_product", apply("root_pivot", root_vector))
    send("root_product", same)
    out_of["root_forward"][...] = total("root_product")
    send("root_forward")
    forward = arrived("root_forward")
    forward = jnp.concatenate([forward[pl.ds(0, 16), :], forward[pl.ds(16, 16), :]], axis=1)
    terms = apply_transposed("root_pivot", forward)
    put("root_terms", terms)
    send("root_terms", lambda place: place % 16)
    stacked("root_rows", terms)
    send("root_rows", same)

    root_blocks = arrived("root_terms")[...]
    out_of["mid_fetch"][...] = pick(mid_place_flip, root_blocks)
    send("mid_fetch", same)
    low_root_part = pick(low_place_root_flip, root_blocks)
    out_of["root_out"][...] = total("root_rows")
    send("root_out")
    out_of["mid_fetched"][...] = total("mid_fetch")
    send("mid_fetched")
    terms = mid_terms - apply_transposed("middle_update", arrived("mid_fetched")[...])
    put("mid_terms", terms)
    send("mid_terms", same)
    for high_part in range(2):
        for low_part in range(2):
            at = (2 * high_part + low_part) * 128
            out_of["mid_rows"][pl.ds(32 * high_part + low_part, 16, stride=2), :] = terms[
                :, at : at + 128
            ]
    send("mid_rows", same)

    out_of["low_fetch"][...] = low_root_part + pick(
        low_place_mid_flip, arrived("mid_terms")[...]
    )
    send("low_fetch", same)
    done = arrived("root_out")
    chosen = lax.broadcasted_iota(jnp.int32, (16, 128), 0) == i16
    for q in range(2):
        block = done[pl.ds(16 * q, 16), :]
        root_solution[0, 0, q] = block
        out_of["root_chain"][pl.ds(q, 1), :] = jnp.sum(
            jnp.where(chosen, block, 0.0), axis=0, keepdims=True
        )
    send("root_chain")
    out_of["mid_out"][...] = total("mid_rows")
    send("mid_out")
    leaf_part = pick(leaf_place_root_flip, arrived("root_chain")[...])
    out_of["low_fetched"][...] = total("low_fetch")
    send("low_fetched")
    terms = low_terms - apply_transposed("lower_update", wide(arrived("low_fetched"), 2))
    put("low_rows", terms)
    send("low_rows", same)
    done = arrived("mid_out")
    for q in range(4):
        block = done[pl.ds(32 * (q // 2) + q % 2, 16, stride=2), :]
        middle_solution[0, 0, q] = block
        out_of["mid_chain"][pl.ds(q, 1), :] = jnp.sum(
            jnp.where(chosen, block, 0.0), axis=0, keepdims=True
        )
    send("mid_chain")
    leaf_part = leaf_part + pick(leaf_place_mid_flip, arrived("mid_chain")[...])

    finished = total("low_rows")
    out_of["low_chain"][...] = finished
    send("low_chain")
    out_of["low_out"][...] = finished
    send("low_out")
    out_of["leaf_fetch"][...] = leaf_part + pick(
        leaf_place_low_flip, arrived("low_chain")[...]
    )
    send("leaf_fetch", same)
    done = arrived("low_out")
    for q in range(4):
        lower_solution[0, 0, q] = done[pl.ds(q, 16, stride=4), :]
    answer = leaf_terms - apply_transposed("leaf_update", wide(arrived("leaf_fetch"), 4))
    leaf_solution[0, 0, 0] = answer[:, :128]
    leaf_solution[0, 0, 1] = answer[:, 128:]

    for index, name in enumerate(NAMES):
        kind, rows = PHASES[name]
        gone = into[name].at[pl.ds(0, (COUNT[kind] - 1) * rows)]
        pltpu.make_async_copy(gone, gone, send_sem.at[index]).wait()


def local(
    leaf_source,
    leaf_pivot,
    leaf_update,
    leaf_targets,
    root_source,
    middle_source,
    lower_source,
    root_pivot,
    middle_pivot,
    lower_pivot,
    middle_update,
    lower_update,
    middle_targets,
    lower_targets,
):
    matrices = {
        "leaf_update": leaf_update,
        "leaf_pivot": leaf_pivot,
        "lower_update": lower_update,
        "lower_pivot": lower_pivot,
        "middle_update": middle_update,
        "middle_pivot": middle_pivot,
        "root_pivot": root_pivot,
    }
    in_vmem = pl.BlockSpec(memory_space=pltpu.VMEM)
    in_smem = pl.BlockSpec(memory_space=pltpu.SMEM)
    anywhere = pl.BlockSpec(memory_space=pl.ANY)
    shapes = list(MATRICES.values())
    return pl.pallas_call(
        kernel,
        out_shape=tuple(
            jax.ShapeDtypeStruct((1, 1, blocks, 16, 128), F32) for blocks in (2, 4, 4, 2)
        ),
        in_specs=[in_vmem, in_smem] + [in_vmem] * 5 + [anywhere] * 7,
        out_specs=(in_vmem,) * 4,
        scratch_shapes=[pltpu.VMEM(shape, F32) for shape in shapes]
        + [pltpu.VMEM(shape, BF16) for shape in shapes] * 2
        + [pltpu.VMEM((SOURCES_OF[name], 128), F32) for name in NAMES]
        + [pltpu.VMEM((COUNT[PHASES[name][0]] * PHASES[name][1], 128), F32) for name in NAMES]
        + [
            pltpu.SemaphoreType.DMA((len(NAMES),)),
            pltpu.SemaphoreType.DMA((len(NAMES),)),
            pltpu.SemaphoreType.DMA((7,)),
        ],
        compiler_params=pltpu.CompilerParams(
            collective_id=0, has_side_effects=True, vmem_limit_bytes=40 * 1024 * 1024
        ),
    )(
        leaf_source,
        leaf_targets,
        root_source,
        middle_source,
        lower_source,
        middle_targets,
        lower_targets,
        *[matrices[name] for name in MATRICES],
    )


def solution(mesh):
    placed = (
        P("row", "col", None, None, None),
        P("row", "col"),
        P("row", "col"),
        P("row", "col", None),
        P("row", "col", None, None),
        P("row", "col", None, None),
        P("row", "col", None, None),
        P("row", "col"),
        P("row", "col"),
        P("row", "col"),
        P("row", "col"),
        P("row", "col"),
        P(),
        P(),
    )
    return jax.shard_map(
        local,
        mesh=mesh,
        in_specs=placed,
        out_specs=(P("row", "col", None, None, None),) * 4,
        check_vma=False,
    )
```

time: 1810 us -> 193 us (0.11)
  waiting for transfers between devices: 1240 us -> 0 us
  blocking collectives: 525 us -> 0 us
  Pallas kernels: 0 us -> 177 us
    psum x3 -> x0, waiting for transfers between devices: 624 us -> none  [the longest x2 454 us: row_total(): lax.psum(slotted(operand, lax.axis_size('row') // group_rows, slot_index)...]
    psum x5 -> x0, blocking collectives: 471 us -> none  [the longest x4 324 us: row_total(): lax.psum(slotted(operand, lax.axis_size('row') // group_rows, slot_index)...]
    reduce_scatter x3 -> x0, waiting for transfers between devices: 427 us -> none  [reduce_level(): lax.psum_scatter(operand.reshape(col_count * col_tiles, source_count, blo...]
    all_gather x2 -> x0, waiting for transfers between devices: 185 us -> none  [spread_columns(): gathered = lax.all_gather(solution, 'col', axis=0, tiled=True)]
    pallas_call x0 -> x1, Pallas kernels: none -> 177 us  [local(): pl.pallas_call(kernel, out_shape=tuple((jax.ShapeDtypeStruct((1, 1, block...]
    all_gather x1 -> x0, blocking collectives: 54.5 us -> none  [spread_columns(): gathered = lax.all_gather(solution, 'col', axis=0, tiled=True)]
  transfers between devices with their start and end apart: 8 -> 0, of which waited for: 8 -> 0; matrix products, arithmetic and copies ran while one was open for 1% -> 0% of each run, Pallas kernels for 0% -> 0%
where the time goes in v1:
time: 193 us; the launch traced here: 192 us
  Pallas kernels  177 us (92%)
  local copies, waits for them, and re-layouts  14.4 us (7%)
    pallas_call x1, Pallas kernels, local(): pl.pallas_call(kernel, out_shape=tuple((jax.ShapeDtypeStruct((1, 1, block...  177 us
    unnamed x32, local copies, waits for them, and re-layouts  14.4 us

profile of v1, /device:TPU:1, one launch (start us, length us, event | category | flops | bytes accessed | tf_op | source)
XLA Modules:
  0.0 192.1 jit_solution(11052947465372193984)
XLA Ops:
  0.6 0.0 copy-start
  0.6 1.2 copy-done
  1.9 0.0 copy-start.1
  1.9 1.0 copy-done.1
  2.9 0.0 copy-start.2
  2.9 1.0 copy-done.2
  3.9 0.0 copy-start.3
  3.9 1.0 copy-done.3
  5.0 0.0 copy-start.4
  5.0 0.9 copy-done.4
  5.9 0.0 copy-start.5
  5.9 0.9 copy-done.5
  6.9 0.0 copy-start.6
  6.9 0.9 copy-done.6
  7.8 0.0 copy-start.7
  7.8 0.7 copy-done.7
  8.6 0.0 copy-start.8
  8.6 0.7 copy-done.8
  9.2 0.0 copy-start.9
  9.2 0.7 copy-done.9
  9.9 0.0 copy-start.10
  9.9 0.7 copy-done.10
  10.6 0.0 copy-start.11
  10.6 0.7 copy-done.11
  11.3 0.0 copy-start.12
  11.3 0.7 copy-done.12
  12.0 0.7 copy-done.13
  12.6 177.0 %shard_map.165 = (f32[1,1,2,16,128]{4,3,2,1,0:T(8,128)S(1)}, f32[1,1,4,16,128]{4,3,2,1,0:T(8,128)S(1)}, f32[1,1,4,16,128]{4,3,2,1,0:T(8,128)S(1)}, f32[1,1,2,16,128]{4,3,2,1,0:T(8,128)S(1)}) custom-call(f32[1,1,2,16,128]{4,3,2,1,0:T(8,128)S(1)} %copy-done.7, s32[1,1,4]{2,1,0:T(1,128)S(1)} %copy-done.13, f32[1,1,2,64]{3,2,1,0:T(2,128)S(1)} %copy-done.11, ...), custom_call_target="tpu_custom_call" | custom-call | tf_op jit(solution)/shard_map/pallas_call | solution.py:534
  189.7 0.6 copy.22
  190.3 0.6 copy.23
  190.9 0.6 copy.24
  191.5 0.6 copy.25
  (1 shorter events, 0.0 us)
Async XLA Ops:
  0.6 1.2 copy-start
  1.9 1.0 copy-start.1
  2.9 1.0 copy-start.2
  3.9 1.0 copy-start.3
  5.0 0.9 copy-start.4
  5.9 0.9 copy-start.5
  6.9 0.9 copy-start.6
  7.8 0.7 copy-start.7
  8.6 0.7 copy-start.8
  9.2 0.7 copy-start.9
  9.9 0.7 copy-start.10
  10.6 0.7 copy-start.11
  11.3 0.7 copy-start.12
  12.0 0.7 copy-start.13

commit v2 on v1

v2 whole, which is shorter than its diff:
```python
import jax
import jax.numpy as jnp
from jax import lax
from jax.experimental import pallas as pl
from jax.experimental.pallas import tpu as pltpu
from jax.sharding import PartitionSpec as P

MESH = pl.DeviceIdType.MESH
F32 = jnp.float32
BF16 = jnp.bfloat16

ROW16, ROW32, COL16, COL32, INWARD, OUTWARD, OUTWARD_ALL = range(7)
(
    TARGETS,
    LEAF_SEND,
    MIDDLE_SOURCE,
    ROOT_SOURCE,
    LOW_BASE,
    LOW_SUM,
    MID_SUM,
    ROOT_SUM,
    LOW_INPUT,
    MID_BASE,
    ROOT_BASE,
    LOW_UPDATE,
    LOW_PRODUCT,
    LOW_FORWARD,
    LOW_SPREAD,
    MID_INPUT,
    MID_UPDATE,
    MID_PRODUCT,
    MID_FORWARD,
    MID_SPREAD,
    ROOT_INPUT,
    ROOT_PRODUCT,
    ROOT_FORWARD,
    ROOT_TERMS,
    MID_FETCH,
    MID_FETCHED,
    ROOT_ROWS,
    ROOT_OUT,
    ROOT_CHAIN,
    MID_TERMS,
    LOW_FETCH,
    LOW_FETCHED,
    MID_ROWS,
    MID_OUT,
    MID_CHAIN,
    LOW_ROWS,
    LOW_CHAIN,
    LOW_OUT,
    LEAF_FETCH,
) = range(39)
(
    LEAF_UPDATE_TILE,
    LEAF_PIVOT_TILE,
    LOWER_UPDATE_TILE,
    LOWER_PIVOT_TILE,
    MIDDLE_UPDATE_TILE,
    MIDDLE_PIVOT_TILE,
    ROOT_PIVOT_TILE,
) = range(7)

PHASES = {
    TARGETS: (ROW16, 1),
    LEAF_SEND: (INWARD, 8),
    MIDDLE_SOURCE: (ROW32, 2),
    ROOT_SOURCE: (ROW32, 1),
    LOW_BASE: (ROW16, 4),
    LOW_SUM: (COL16, 8),
    MID_SUM: (COL16, 8),
    ROOT_SUM: (COL32, 4),
    LOW_INPUT: (OUTWARD, 8),
    MID_BASE: (OUTWARD_ALL, 8),
    ROOT_BASE: (OUTWARD_ALL, 4),
    LOW_UPDATE: (COL16, 2),
    LOW_PRODUCT: (COL16, 4),
    LOW_FORWARD: (COL16, 4),
    LOW_SPREAD: (ROW32, 2),
    MID_INPUT: (COL16, 4),
    MID_UPDATE: (COL16, 1),
    MID_PRODUCT: (COL16, 2),
    MID_FORWARD: (COL16, 2),
    MID_SPREAD: (ROW32, 1),
    ROOT_INPUT: (COL32, 2),
    ROOT_PRODUCT: (COL32, 1),
    ROOT_FORWARD: (COL32, 1),
    ROOT_TERMS: (COL32, 2),
    MID_FETCH: (ROW32, 1),
    MID_FETCHED: (COL16, 1),
    ROOT_ROWS: (ROW32, 1),
    ROOT_OUT: (ROW32, 1),
    ROOT_CHAIN: (COL32, 4),
    MID_TERMS: (COL16, 4),
    LOW_FETCH: (ROW32, 2),
    LOW_FETCHED: (COL16, 2),
    MID_ROWS: (ROW32, 2),
    MID_OUT: (ROW32, 2),
    MID_CHAIN: (COL16, 8),
    LOW_ROWS: (INWARD, 8),
    LOW_CHAIN: (COL16, 8),
    LOW_OUT: (OUTWARD, 8),
    LEAF_FETCH: (OUTWARD, 8),
}
NAMES = list(PHASES)
COUNT = {ROW16: 16, ROW32: 32, COL16: 16, COL32: 32, INWARD: 16, OUTWARD: 8, OUTWARD_ALL: 16}
CENTRAL = (LOW_SUM, MID_SUM, ROOT_SUM, ROOT_CHAIN, MID_CHAIN, LOW_CHAIN)

SOURCES_OF = {
    TARGETS: 1,
    LEAF_SEND: 64,
    MIDDLE_SOURCE: 2,
    ROOT_SOURCE: 1,
    LOW_BASE: 4,
    LOW_SUM: 128,
    MID_SUM: 128,
    ROOT_SUM: 128,
    LOW_INPUT: 8,
    MID_BASE: 8,
    ROOT_BASE: 4,
    LOW_UPDATE: 32,
    LOW_PRODUCT: 64,
    LOW_FORWARD: 4,
    LOW_SPREAD: 2,
    MID_INPUT: 64,
    MID_UPDATE: 16,
    MID_PRODUCT: 32,
    MID_FORWARD: 2,
    MID_SPREAD: 1,
    ROOT_INPUT: 64,
    ROOT_PRODUCT: 32,
    ROOT_FORWARD: 1,
    ROOT_TERMS: 32,
    MID_FETCH: 32,
    MID_FETCHED: 1,
    ROOT_ROWS: 32,
    ROOT_OUT: 1,
    ROOT_CHAIN: 4,
    MID_TERMS: 64,
    LOW_FETCH: 64,
    LOW_FETCHED: 2,
    MID_ROWS: 64,
    MID_OUT: 2,
    MID_CHAIN: 8,
    LOW_ROWS: 64,
    LOW_CHAIN: 8,
    LOW_OUT: 8,
    LEAF_FETCH: 128,
}

MATRICES = {
    LEAF_UPDATE_TILE: (512, 256),
    LEAF_PIVOT_TILE: (256, 256),
    LOWER_UPDATE_TILE: (256, 512),
    LOWER_PIVOT_TILE: (512, 512),
    MIDDLE_UPDATE_TILE: (128, 512),
    MIDDLE_PIVOT_TILE: (256, 512),
    ROOT_PIVOT_TILE: (256, 256),
}


def halves(value):
    high = value.astype(BF16)
    return high, (value - high.astype(F32)).astype(BF16)


def product(vector, high, low, contract):
    vector_high, vector_low = halves(vector)
    dims = (((1,), (contract,)), ((), ()))
    both = lax.dot_general(
        jnp.concatenate([vector_high, vector_low], axis=0), high, dims, preferred_element_type=F32
    )
    rest = lax.dot_general(vector_high, low, dims, preferred_element_type=F32)
    return both[:16] + (both[16:] + rest)


def pick(selector, blocks):
    high, low = halves(blocks)
    return jnp.dot(selector, high, preferred_element_type=F32) + jnp.dot(
        selector, low, preferred_element_type=F32
    )


def as_float(condition):
    return jnp.where(condition, 1.0, 0.0).astype(BF16)


def flipped(selector):
    count = selector.shape[1]
    rows = lax.broadcasted_iota(jnp.int32, (count, count), 0)
    cols = lax.broadcasted_iota(jnp.int32, (count, count), 1)
    return lax.dot_general(
        as_float(rows == cols), selector, (((1,), (1,)), ((), ())), preferred_element_type=F32
    ).astype(BF16)


def root_numbers(width):
    slot = lax.broadcasted_iota(jnp.int32, (64, width), 0)
    return (slot & 1) * 32 + (slot >> 1)


def group_numbers(width):
    slot = lax.broadcasted_iota(jnp.int32, (64, width), 0)
    return (slot & 3) * 16 + (slot >> 2)


def kernel(*rest):
    small_hbm = rest[:7]
    in_hbm = dict(zip(MATRICES, rest[7:14]))
    root_solution, middle_solution, lower_solution, leaf_solution = rest[14:18]
    small = rest[18:25]
    leaf_source, leaf_targets, root_source, middle_source, lower_source = small[:5]
    middle_targets, lower_targets = small[5:]
    rest = rest[25:]
    loaded = dict(zip(MATRICES, rest[:7]))
    high = dict(zip(MATRICES, rest[7:14]))
    low = dict(zip(MATRICES, rest[14:21]))
    rest = rest[21:]
    out_of = dict(zip(NAMES, rest[: len(NAMES)]))
    into = dict(zip(NAMES, rest[len(NAMES) : 2 * len(NAMES)]))
    tally, send_sem, recv_sem, load_sem = rest[2 * len(NAMES) :]

    r = lax.axis_index("row")
    c = lax.axis_index("col")
    half = c // 16
    i16 = r % 16
    j16 = c % 16
    core, x, y = lax.rem(c, 2), lax.rem(c // 2, 4), c // 8
    low_y = lax.rem(y, 2)
    back = i16 // 8
    own = i16 * back + (15 - i16) * (1 - back)
    central = jnp.logical_and(i16 >= 4, i16 < 12)
    my_place = {ROW16: i16, ROW32: r, COL16: j16, COL32: c}

    def peer(kind, step):
        if kind == ROW32:
            odd = lax.rem(step, 2)
            place = lax.rem(r + 16 + (2 * odd - 1) * lax.div(step + 1, 2), 32)
            return place, (place, c)
        if kind == ROW16:
            at = step + jnp.where(step >= own, 1, 0)
            place = at * back + (15 - at) * (1 - back)
            return place, (r - i16 + place, c)
        if kind == COL16:
            at = step + jnp.where(step >= 13, 1, 0)
            place = (
                lax.rem(low_y + 1 + lax.div(at, 8), 2) * 8
                + lax.rem(x + 2 + lax.div(at, 2), 4) * 2
                + lax.rem(core + 1 + at, 2)
            )
            return place, (r, half * 16 + place)
        at = step + jnp.where(step >= 21, 1, 0)
        place = (
            lax.rem(y + 2 + lax.div(at, 8), 4) * 8
            + lax.rem(x + 2 + lax.div(at, 2), 4) * 2
            + lax.rem(core + 1 + at, 2)
        )
        return place, (r, place)

    def each_peer(kind, act):
        lax.fori_loop(0, COUNT[kind] - 1, act, 0)

    def send(name, each=None):
        kind, rows = PHASES[name]
        index = NAMES.index(name)
        source, target = out_of[name], into[name]

        def piece(place):
            return source.at[pl.ds(0 if each is None else each(place) * rows, rows)]

        here = target.at[pl.ds(my_place[kind] * rows, rows)]

        def one(step, carry):
            place, device = peer(kind, step)
            pltpu.make_async_remote_copy(
                src_ref=piece(place),
                dst_ref=here,
                send_sem=send_sem.at[index],
                recv_sem=recv_sem.at[index],
                device_id=device,
                device_id_type=MESH,
            ).start()
            return carry

        each_peer(kind, one)
        pltpu.make_async_copy(piece(my_place[kind]), here, recv_sem.at[index]).start()

    def remote(name, source, target, device):
        index = NAMES.index(name)
        pltpu.make_async_remote_copy(
            src_ref=source,
            dst_ref=target,
            send_sem=send_sem.at[index],
            recv_sem=recv_sem.at[index],
            device_id=device,
            device_id_type=MESH,
        ).start()

    def inward(name):
        source, target = out_of[name], into[name]
        here = target.at[pl.ds(i16 * 8, 8)]

        def one(step, carry):
            at = step * back + (7 - step) * (1 - back)

            @pl.when(at + 4 != i16)
            def _():
                remote(name, source.at[pl.ds(at * 8, 8)], here, (r - i16 + 4 + at, c))

            return carry

        lax.fori_loop(0, 8, one, 0)

        @pl.when(central)
        def _():
            pltpu.make_async_copy(
                source.at[pl.ds((i16 - 4) * 8, 8)], here, recv_sem.at[NAMES.index(name)]
            ).start()

    def outward(name, each=None):
        kind, rows = PHASES[name]
        source, target = out_of[name], into[name]

        def piece(place):
            return source.at[pl.ds(0 if each is None else each(place) * rows, rows)]

        if kind == OUTWARD_ALL:
            here = target.at[pl.ds((r // 16 * 8 + i16 - 4) * rows, rows)]

            def one(step, carry):
                place, device = peer(ROW32, step)
                remote(name, piece(place), here, device)
                return carry

            lax.fori_loop(0, 31, one, 0)
            own_piece = piece(r)
        else:
            here = target.at[pl.ds((i16 - 4) * rows, rows)]

            def one(step, carry):
                place, device = peer(ROW16, step)
                remote(name, piece(place), here, device)
                return carry

            lax.fori_loop(0, 15, one, 0)
            own_piece = piece(i16)
        pltpu.make_async_copy(own_piece, here, recv_sem.at[NAMES.index(name)]).start()

    def arrived(name):
        buffer = into[name]
        pltpu.make_async_copy(buffer, buffer, recv_sem.at[NAMES.index(name)]).wait()
        return buffer

    def total(name):
        kind, rows = PHASES[name]
        buffer = arrived(name)
        parts = [buffer[pl.ds(8 * at, 8), :] for at in range(COUNT[kind] * rows // 8)]
        while len(parts) > 1:
            parts = [a + b for a, b in zip(parts[::2], parts[1::2])]
        value = parts[0]
        size = 8
        while size > rows:
            size //= 2
            value = value[:size] + value[size:]
        return value

    def wide(buffer, rows, start=0):
        return jnp.concatenate(
            [buffer[pl.ds(start + at, 16, stride=rows), :] for at in range(rows)], axis=1
        )

    def put(name, value):
        rows = value.shape[1] // 128
        buffer = out_of[name]
        if rows == 1:
            buffer[...] = value
        else:
            for at in range(rows):
                buffer[pl.ds(at, 16, stride=rows), :] = value[:, at * 128 : (at + 1) * 128]

    def stacked(name, value):
        for at in range(value.shape[1] // 128):
            out_of[name][pl.ds(at * 16, 16), :] = value[:, at * 128 : (at + 1) * 128]

    def load(name):
        index = list(MATRICES).index(name)
        return pltpu.make_async_copy(in_hbm[name], loaded[name], load_sem.at[index])

    def split(name):
        load(name).wait()
        high[name][...], low[name][...] = halves(loaded[name][...])

    def apply(name, vector):
        return product(vector, high[name][...], low[name][...], 1)

    def apply_transposed(name, vector):
        return product(vector, high[name][...], low[name][...], 0)

    same = lambda place: place

    def load_small(index):
        return pltpu.make_async_copy(small_hbm[index], small[index], load_sem.at[7 + index])

    load_small(0).start()
    load_small(1).start()
    for name in MATRICES:
        load(name).start()
    for index in range(2, 7):
        load_small(index).start()

    barrier = pltpu.get_barrier_semaphore()
    for kind in (ROW32, COL32):

        def greet(step, carry, kind=kind):
            pl.semaphore_signal(
                barrier, inc=1, device_id=peer(kind, step)[1], device_id_type=MESH
            )
            return carry

        each_peer(kind, greet)

    for index in range(7):
        load_small(index).wait()
    lane = lax.broadcasted_iota(jnp.int32, (4, 128), 1)
    entry = lax.broadcasted_iota(jnp.int32, (4, 128), 0)
    own_lane = jnp.logical_and(lane >> 3 == i16, lane & 3 == entry)
    own_targets = jnp.broadcast_to(leaf_targets[0].astype(F32), (8, 4)).astype(BF16)
    out_of[TARGETS][...] = jnp.dot(
        own_targets, as_float(own_lane), preferred_element_type=F32
    )[0:1]
    mid_src = middle_source[0, 0]
    out_of[MIDDLE_SOURCE][...] = jnp.concatenate(
        [
            jnp.concatenate([mid_src[0:1], mid_src[1:2]], axis=1),
            jnp.concatenate([mid_src[2:3], mid_src[3:4]], axis=1),
        ],
        axis=0,
    )
    root_src = root_source[0, 0]
    out_of[ROOT_SOURCE][...] = jnp.concatenate([root_src[0:1], root_src[1:2]], axis=1)

    leaf_vector = jnp.concatenate([leaf_source[0, 0, 0], leaf_source[0, 0, 1]], axis=1)
    split(LEAF_UPDATE_TILE)
    put(LEAF_SEND, apply(LEAF_UPDATE_TILE, leaf_vector))

    pl.semaphore_wait(barrier, 62)
    inward(LEAF_SEND)
    send(TARGETS)
    out_of[LOW_BASE][...] = lower_source[0, 0]

    for name in list(MATRICES)[1:]:
        split(name)
    leaf_terms = apply_transposed(LEAF_PIVOT_TILE, apply(LEAF_PIVOT_TILE, leaf_vector))

    mid_target = middle_targets[pl.ds(half, 1), :]
    mid_place = as_float(root_numbers(32) == mid_target)
    mid_place_flip = flipped(mid_place)
    update_row = lax.broadcasted_iota(jnp.int32, (32, 64), 0)
    slot = lax.broadcasted_iota(jnp.int32, (32, 64), 1)
    order = (update_row & 15) * 2 + (update_row >> 4)
    low_target = jnp.zeros((8, 64), F32)
    for part in range(2):
        values = lower_targets[pl.ds(2 * half + part, 1), :].astype(F32)
        low_target = low_target + jnp.dot(
            jnp.broadcast_to(values, (8, 32)).astype(BF16),
            as_float(slot == order + 32 * part),
            preferred_element_type=F32,
        )
    low_target = low_target[0:1]
    low_place_root = as_float(root_numbers(64).astype(F32) == low_target)
    low_place_mid = as_float((group_numbers(64) + 64).astype(F32) == low_target)
    low_place_root_flip = flipped(low_place_root)
    low_place_mid_flip = flipped(low_place_mid)

    send(LOW_BASE)

    lane = lax.broadcasted_iota(jnp.int32, (1, 128), 1)
    leaf_target = jnp.sum(arrived(TARGETS)[...], axis=0, keepdims=True)
    leaf_target = leaf_target + ((lane >> 2 & 1) * 256).astype(F32)
    slot = lax.broadcasted_iota(jnp.int32, (128, 128), 0)
    group_number = (slot & 3) * 16 + (slot >> 3) + (slot >> 2 & 1) * 256
    root_number = (slot & 1) * 32 + (slot >> 2) + (slot >> 1 & 1) * 256
    leaf_place_low = as_float((group_number + 128).astype(F32) == leaf_target)
    leaf_place_mid = as_float((group_number + 64).astype(F32) == leaf_target)
    leaf_place_root = as_float(root_number.astype(F32) == leaf_target)

    @pl.when(central)
    def _():
        sent = arrived(LEAF_SEND)[...]
        out_of[LOW_SUM][...] = pick(leaf_place_low, sent)
        send(LOW_SUM, same)
        out_of[MID_SUM][...] = pick(leaf_place_mid, sent)
        send(MID_SUM, same)
        out_of[LOW_INPUT][...] = total(LOW_SUM)
        outward(LOW_INPUT)
        out_of[ROOT_SUM][...] = pick(leaf_place_root, sent)
        send(ROOT_SUM, same)
        out_of[MID_BASE][...] = total(MID_SUM)
        outward(MID_BASE)
        out_of[ROOT_BASE][...] = total(ROOT_SUM)

    leaf_place_low_flip = flipped(leaf_place_low)
    leaf_place_mid_flip = flipped(leaf_place_mid)
    leaf_place_root_flip = flipped(leaf_place_root)

    low_base = wide(arrived(LOW_BASE), 4)
    low_vector = low_base - wide(arrived(LOW_INPUT), 4)
    put(LOW_UPDATE, apply(LOWER_UPDATE_TILE, low_vector))
    send(LOW_UPDATE, same)
    send(MIDDLE_SOURCE)
    put(LOW_PRODUCT, apply(LOWER_PIVOT_TILE, low_vector))
    out_of[LOW_SPREAD][...] = total(LOW_UPDATE)
    send(LOW_SPREAD)
    send(LOW_PRODUCT, same)
    out_of[LOW_FORWARD][...] = total(LOW_PRODUCT)
    send(LOW_FORWARD)
    upper_lane = lax.broadcasted_iota(jnp.int32, (16, 128), 1) >= 64
    source_rows = arrived(MIDDLE_SOURCE)
    mid_base = []
    for pair in range(2):
        even = source_rows[pl.ds(pair, 16, stride=4), :]
        odd = source_rows[pl.ds(2 + pair, 16, stride=4), :]
        mid_base.append(jnp.where(upper_lane, pltpu.roll(odd, 64, 1), even))
        mid_base.append(jnp.where(upper_lane, odd, pltpu.roll(even, 64, 1)))
    sums = arrived(MID_BASE)
    mid_base = jnp.concatenate(mid_base, axis=1) - (wide(sums, 4) + wide(sums, 4, 64))
    low_terms = apply_transposed(LOWER_PIVOT_TILE, wide(arrived(LOW_FORWARD), 4))

    updates = arrived(LOW_SPREAD)[...]
    out_of[MID_INPUT][...] = pick(low_place_mid, updates)
    send(MID_INPUT, same)

    @pl.when(central)
    def _():
        outward(ROOT_BASE)

    send(ROOT_SOURCE)
    root_updates = pick(low_place_root, updates)
    mid_vector = mid_base - wide(arrived(MID_INPUT), 4)
    put(MID_UPDATE, apply(MIDDLE_UPDATE_TILE, mid_vector))
    send(MID_UPDATE, same)
    put(MID_PRODUCT, apply(MIDDLE_PIVOT_TILE, mid_vector))
    out_of[MID_SPREAD][...] = total(MID_UPDATE)
    send(MID_SPREAD)
    send(MID_PRODUCT, same)
    out_of[MID_FORWARD][...] = total(MID_PRODUCT)
    send(MID_FORWARD)
    source_rows = arrived(ROOT_SOURCE)
    even = source_rows[pl.ds(0, 16, stride=2), :]
    odd = source_rows[pl.ds(1, 16, stride=2), :]
    root_base = jnp.concatenate(
        [
            jnp.where(upper_lane, pltpu.roll(odd, 64, 1), even),
            jnp.where(upper_lane, odd, pltpu.roll(even, 64, 1)),
        ],
        axis=1,
    )
    sums = arrived(ROOT_BASE)
    root_base = root_base - (wide(sums, 2) + wide(sums, 2, 32))
    mid_terms = apply_transposed(MIDDLE_PIVOT_TILE, wide(arrived(MID_FORWARD), 2))

    out_of[ROOT_INPUT][...] = root_updates + pick(mid_place, arrived(MID_SPREAD)[...])
    send(ROOT_INPUT, same)
    sums = arrived(ROOT_INPUT)
    root_vector = root_base - (wide(sums, 2) + wide(sums, 2, 32))
    stacked(ROOT_PRODUCT, apply(ROOT_PIVOT_TILE, root_vector))
    send(ROOT_PRODUCT, same)
    out_of[ROOT_FORWARD][...] = total(ROOT_PRODUCT)
    send(ROOT_FORWARD)
    forward = arrived(ROOT_FORWARD)
    forward = jnp.concatenate([forward[pl.ds(0, 16), :], forward[pl.ds(16, 16), :]], axis=1)
    terms = apply_transposed(ROOT_PIVOT_TILE, forward)
    put(ROOT_TERMS, terms)
    send(ROOT_TERMS, lambda place: place % 16)
    stacked(ROOT_ROWS, terms)
    send(ROOT_ROWS, same)

    root_blocks = arrived(ROOT_TERMS)[...]
    out_of[MID_FETCH][...] = pick(mid_place_flip, root_blocks)
    send(MID_FETCH, same)
    low_root_part = pick(low_place_root_flip, root_blocks)
    out_of[ROOT_OUT][...] = total(ROOT_ROWS)
    send(ROOT_OUT)
    out_of[MID_FETCHED][...] = total(MID_FETCH)
    send(MID_FETCHED)
    terms = mid_terms - apply_transposed(MIDDLE_UPDATE_TILE, arrived(MID_FETCHED)[...])
    put(MID_TERMS, terms)
    send(MID_TERMS, same)
    for high_part in range(2):
        for low_part in range(2):
            at = (2 * high_part + low_part) * 128
            out_of[MID_ROWS][pl.ds(32 * high_part + low_part, 16, stride=2), :] = terms[
                :, at : at + 128
            ]
    send(MID_ROWS, same)

    out_of[LOW_FETCH][...] = low_root_part + pick(
        low_place_mid_flip, arrived(MID_TERMS)[...]
    )
    send(LOW_FETCH, same)
    done = arrived(ROOT_OUT)
    row_number = lax.broadcasted_iota(jnp.int32, (16, 128), 0)
    for q in range(2):
        root_solution[0, 0, q] = done[pl.ds(16 * q, 16), :]

    def own_source(block, which):
        chosen = row_number == 2 * (i16 - 4) + which
        return jnp.sum(jnp.where(chosen, block, 0.0), axis=0, keepdims=True)

    @pl.when(central)
    def _():
        for q in range(2):
            for which in range(2):
                out_of[ROOT_CHAIN][pl.ds(2 * which + q, 1), :] = own_source(
                    into[ROOT_OUT][pl.ds(16 * q, 16), :], which
                )
        send(ROOT_CHAIN)

    out_of[MID_OUT][...] = total(MID_ROWS)
    send(MID_OUT)

    @pl.when(central)
    def _():
        out_of[LEAF_FETCH][...] = pick(leaf_place_root_flip, arrived(ROOT_CHAIN)[...])

    out_of[LOW_FETCHED][...] = total(LOW_FETCH)
    send(LOW_FETCHED)
    terms = low_terms - apply_transposed(LOWER_UPDATE_TILE, wide(arrived(LOW_FETCHED), 2))
    put(LOW_ROWS, terms)
    inward(LOW_ROWS)
    done = arrived(MID_OUT)
    for q in range(4):
        middle_solution[0, 0, q] = done[pl.ds(32 * (q // 2) + q % 2, 16, stride=2), :]

    @pl.when(central)
    def _():
        for q in range(4):
            for which in range(2):
                out_of[MID_CHAIN][pl.ds(4 * which + q, 1), :] = own_source(
                    into[MID_OUT][pl.ds(32 * (q // 2) + q % 2, 16, stride=2), :], which
                )
        send(MID_CHAIN)
        finished = total(LOW_ROWS)
        out_of[LOW_CHAIN][...] = finished
        send(LOW_CHAIN)
        out_of[LOW_OUT][...] = finished
        outward(LOW_OUT)
        out_of[LEAF_FETCH][...] += pick(leaf_place_mid_flip, arrived(MID_CHAIN)[...])
        out_of[LEAF_FETCH][...] += pick(leaf_place_low_flip, arrived(LOW_CHAIN)[...])
        outward(LEAF_FETCH, same)

    done = arrived(LOW_OUT)
    for q in range(4):
        lower_solution[0, 0, q] = done[pl.ds(q, 16, stride=4), :]
    answer = leaf_terms - apply_transposed(LEAF_UPDATE_TILE, wide(arrived(LEAF_FETCH), 4))
    leaf_solution[0, 0, 0] = answer[:, :128]
    leaf_solution[0, 0, 1] = answer[:, 128:]

    def gone(name, rows):
        buffer = tally.at[pl.ds(0, rows)]
        pltpu.make_async_copy(buffer, buffer, send_sem.at[NAMES.index(name)]).wait()

    for name in NAMES:
        kind, rows = PHASES[name]
        if kind not in (INWARD, OUTWARD, OUTWARD_ALL) and name not in CENTRAL:
            gone(name, (COUNT[kind] - 1) * rows)

    @pl.when(central)
    def _():
        for name in NAMES:
            kind, rows = PHASES[name]
            if name in CENTRAL:
                gone(name, (COUNT[kind] - 1) * rows)
            elif kind == INWARD:
                gone(name, 7 * rows)
            elif kind == OUTWARD:
                gone(name, 15 * rows)
            elif kind == OUTWARD_ALL:
                gone(name, 31 * rows)

    @pl.when(jnp.logical_not(central))
    def _():
        for name in NAMES:
            kind, rows = PHASES[name]
            if kind == INWARD:
                gone(name, 8 * rows)


def local(
    leaf_source,
    leaf_pivot,
    leaf_update,
    leaf_targets,
    root_source,
    middle_source,
    lower_source,
    root_pivot,
    middle_pivot,
    lower_pivot,
    middle_update,
    lower_update,
    middle_targets,
    lower_targets,
):
    matrices = {
        LEAF_UPDATE_TILE: leaf_update,
        LEAF_PIVOT_TILE: leaf_pivot,
        LOWER_UPDATE_TILE: lower_update,
        LOWER_PIVOT_TILE: lower_pivot,
        MIDDLE_UPDATE_TILE: middle_update,
        MIDDLE_PIVOT_TILE: middle_pivot,
        ROOT_PIVOT_TILE: root_pivot,
    }
    in_vmem = pl.BlockSpec(memory_space=pltpu.VMEM)
    in_hbm = pl.BlockSpec(memory_space=pltpu.HBM)
    small = (
        leaf_source,
        leaf_targets,
        root_source,
        middle_source,
        lower_source,
        middle_targets,
        lower_targets,
    )
    shapes = list(MATRICES.values())
    return pl.pallas_call(
        kernel,
        out_shape=tuple(
            jax.ShapeDtypeStruct((1, 1, blocks, 16, 128), F32) for blocks in (2, 4, 4, 2)
        ),
        in_specs=[in_hbm] * 14,
        out_specs=(in_vmem,) * 4,
        scratch_shapes=[pltpu.VMEM(array.shape, array.dtype) for array in small]
        + [pltpu.VMEM(shape, F32) for shape in shapes]
        + [pltpu.VMEM(shape, BF16) for shape in shapes] * 2
        + [pltpu.VMEM((SOURCES_OF[name], 128), F32) for name in NAMES]
        + [pltpu.VMEM((COUNT[PHASES[name][0]] * PHASES[name][1], 128), F32) for name in NAMES]
        + [
            pltpu.VMEM((256, 128), F32),
            pltpu.SemaphoreType.DMA((len(NAMES),)),
            pltpu.SemaphoreType.DMA((len(NAMES),)),
            pltpu.SemaphoreType.DMA((14,)),
        ],
        compiler_params=pltpu.CompilerParams(
            collective_id=0, has_side_effects=True, vmem_limit_bytes=60 * 1024 * 1024
        ),
    )(
        *small,
        *[matrices[name] for name in MATRICES],
    )


def solution(mesh):
    placed = (
        P("row", "col", None, None, None),
        P("row", "col"),
        P("row", "col"),
        P("row", "col", None),
        P("row", "col", None, None),
        P("row", "col", None, None),
        P("row", "col", None, None),
        P("row", "col"),
        P("row", "col"),
        P("row", "col"),
        P("row", "col"),
        P("row", "col"),
        P(),
        P(),
    )
    return jax.shard_map(
        local,
        mesh=mesh,
        in_specs=placed,
        out_specs=(P("row", "col", None, None, None),) * 4,
        check_vma=False,
    )
```

time: 193 us -> 173 us (0.90)
  local copies, waits for them, and re-layouts: 14.4 us -> 3.44 us
  Pallas kernels: 177 us -> 168 us
    unnamed x32 -> x10, local copies, waits for them, and re-layouts: 14.4 us -> 3.44 us
    pallas_call x1, Pallas kernels: 177 us -> 168 us  [local(): pl.pallas_call(kernel, out_shape=tuple((jax.ShapeDtypeStruct((1, 1, block...]
where the time goes in v2:
time: 173 us
  Pallas kernels  168 us (97%)
  local copies, waits for them, and re-layouts  3.44 us (2%)
    pallas_call x1, Pallas kernels, local(): pl.pallas_call(kernel, out_shape=tuple((jax.ShapeDtypeStruct((1, 1, block...  168 us

profile of v2, /device:TPU:1, one launch (start us, length us, event | category | flops | bytes accessed | tf_op | source)
XLA Modules:
  0.0 172.6 jit_solution(1848145187025671006)
XLA Ops:
  0.6 168.5 %shard_map.165 = (f32[1,1,2,16,128]{4,3,2,1,0:T(8,128)}, f32[1,1,4,16,128]{4,3,2,1,0:T(8,128)}, f32[1,1,4,16,128]{4,3,2,1,0:T(8,128)}, f32[1,1,2,16,128]{4,3,2,1,0:T(8,128)}) custom-call(f32[1,1,2,16,128]{4,3,2,1,0:T(8,128)} %rest_0_.1, s32[1,1,4]{2,1,0:T(1,128)} %rest_1_.1, f32[1,1,2,64]{3,2,1,0:T(2,128)} %rest_2_.1, f32[1,1,4,64]{3,2,1,0:T(4,128)} %rest_3_.1, ...), custom_call_target="tpu_custom_call" | custom-call | tf_op jit(solution)/shard_map/pallas_call | solution.py:726
  169.1 0.0 copy-start.1
  169.1 1.3 copy.22
  170.4 0.0 copy-done.1
  170.5 0.0 copy-start
  170.5 0.6 copy.23
  171.1 0.2 copy-done
  171.2 0.0 copy-start.2
  171.2 0.6 copy.24
  171.8 0.1 copy-done.2
  172.0 0.6 copy.25
Async XLA Ops:
  169.1 1.3 copy-start.1
  170.5 0.8 copy-start
  171.2 0.7 copy-start.2
